TPU v7x, 32 devices: a whole 2x2x4 slice. The times are simulated.
32 devices in a mesh: groups: 2 (over y), tp: 16 (over z, x, core).
Axes of the slice: x: 2, y: 2, z: 4, core: 2. Of those that a mesh axis runs over, the one named last changes fastest.
Arguments:
- hidden: bfloat16 [64, 26624], P('groups', 'tp'), parts along dimension 0, may hold values from -6 to 6
- down_weight: bfloat16 [26624, 16384], P('tp'), may hold values from -0.0546875 to 0.0546875
- residual: bfloat16 [64, 16384], P('groups', 'tp'), parts along dimension 0, may hold values from -6 to 6
Outputs:
- out_values: bfloat16 [64, 16384], P('groups'), parts along dimension 0
- out_scales: bfloat16 [64, 128], P('groups'), parts along dimension 0
There are 2 independent parts, one for each index of `groups`. A program takes and returns all parts, laid end to end along the dimension named above; an argument that names none is the same for every part. Nothing has to cross between parts.
All inputs are finite; a program needn't handle non-finite values. Where the computation divides by a largest or mean magnitude, that divisor is 1e-20 or more.
Results may differ from a plain program's by a relative error of at most 0.0095.
Values may be sent and summed in bfloat16 or wider, within the bound.
A program may use at most 128 MiB of HBM per device.

v0:
```python
import jax
import jax.numpy as jnp
from jax import lax
from jax.sharding import PartitionSpec as P

BLOCK = 128


def encode(values):
    row_count = values.shape[0]
    width = values.shape[1]
    blocks = values.reshape(row_count, width // BLOCK, BLOCK)
    scale = (jnp.max(jnp.abs(blocks), axis=2) + 1e-06).astype(jnp.bfloat16)
    coded = (blocks / scale.astype(jnp.float32)[:, :, None]).astype(jnp.bfloat16)
    return (coded.reshape(row_count, width), scale)


def decode_sum(received, count, row_count):
    coded, scale = received
    width = coded.shape[1]
    blocks = coded.astype(jnp.float32).reshape(count, row_count, width // BLOCK, BLOCK)
    factors = scale.astype(jnp.float32).reshape(count, row_count, width // BLOCK, 1)
    return jnp.sum(blocks * factors, axis=0).reshape(row_count, width)


def shards(hidden, down_weight, residual):
    count = lax.axis_size("tp")
    row_count = hidden.shape[0]
    term = jnp.dot(hidden, down_weight, preferred_element_type=jnp.float32)
    coded, scale = encode(term)
    got = (
        lax.all_to_all(coded, "tp", split_axis=1, concat_axis=0, tiled=True),
        lax.all_to_all(scale, "tp", split_axis=1, concat_axis=0, tiled=True),
    )
    branch = decode_sum(got, count, row_count)
    summed = residual.astype(jnp.float32) + branch
    local_values, local_scales = encode(summed)
    out_values, out_scales = (
        lax.all_gather(local_values, "tp", axis=1, tiled=True),
        lax.all_gather(local_scales, "tp", axis=1, tiled=True),
    )
    return (out_values, out_scales)


def solution(mesh):
    in_specs = (P("groups", "tp"), P("tp", None), P("groups", "tp"))
    out_specs = (P("groups", None), P("groups", None))
    return jax.shard_map(shards, mesh=mesh, in_specs=in_specs, out_specs=out_specs, check_vma=False)
```

profile of v0, /device:TPU:0, one launch (start us, length us, event | category | flops | bytes accessed | tf_op | source)
XLA Modules:
  0.0 120.8 jit_solution(11383142950976247185)
XLA Ops:
  7.2 0.0 copy-start
  7.2 0.9 copy-done
  8.1 19.6 %fusion.3 = f32[32,16384]{1,0:T(8,128)S(1)} fusion(bf16[32,1664]{1,0:T(8,128)(2,1)S(1)} %copy-done, bf16[1664,16384]{1,0:T(8,128)(2,1)} %param.4), kind=kOutput, calls=%fused_computation.15 | convolution fusion | flops 1744830464 | bytes 56729600 | tf_op jit(solution)/shard_map/dot_general | solution.py:29
  27.6 0.2 abs_bitcast_fusion
  27.8 0.4 copy.24
  28.2 0.6 bitcast_reduce_fusion
  28.8 0.1 copy.18
  29.0 0.7 reshape.42
  29.7 7.4 %all-to-all-start.1 = ((bf16[16,2,128]{2,1,0:T(2,128)(2,1)}), bf16[16,2,128]{2,1,0:T(2,128)(2,1)S(1)}, u32[]{:S(2)}, u32[]{:S(2)}) async-start(bf16[16,2,128]{2,1,0:T(2,128)(2,1)} %reshape.42), calls=%async_computation.1 | async-start | bytes 16384 | tf_op jit(solution)/shard_map/all_to_all | solution.py:33
  37.0 0.6 div.22
  37.6 1.3 %fusion = bf16[32,16384]{1,0:T(8,128)(2,1)S(1)} fusion(f32[32,16384]{1,0:T(8,128)S(1)} %fusion.3, f32[4,8,128,128]{3,2,1,0:T(8,128)S(1)} %bitcast.37), kind=kLoop, calls=%fused_computation.1 | loop fusion | flops 1048576 | bytes 5242880 | tf_op jit(solution)/shard_map/convert_element_type | solution.py:14
  39.0 1.0 copy.31
  40.0 3.4 %all-to-all-done.1 = bf16[16,2,128]{2,1,0:T(2,128)(2,1)S(1)} async-done(((bf16[16,2,128]{2,1,0:T(2,128)(2,1)}), bf16[16,2,128]{2,1,0:T(2,128)(2,1)S(1)}, u32[]{:S(2)}, u32[]{:S(2)}) %all-to-all-start.1) | async-done | bytes 8224 | tf_op jit(solution)/shard_map/all_to_all | solution.py:33
  43.4 3.7 %all-to-all-start = ((bf16[32,16,1024]{2,0,1:T(8,128)(2,1)}), bf16[32,16,1024]{2,0,1:T(8,128)(2,1)S(1)}, u32[]{:S(2)}, u32[]{:S(2)}) async-start(bf16[32,16,1024]{2,0,1:T(8,128)(2,1)} %bitcast.36), calls=%async_computation | async-start | bytes 2097152 | tf_op jit(solution)/shard_map/all_to_all | solution.py:32
  47.0 0.0 all-gather.2.cloned.1.call-start
  47.1 0.1 reshape.43
  47.2 0.1 copy.19
  47.3 2.0 %mul.11 = f32[16,32,8,128]{3,2,1,0:T(8,128)} broadcast(f32[16,32,8]{2,1,0:T(8,128)S(1)} %copy.19), dimensions={0,1,2} | broadcast | bytes 2113536 | tf_op jit(solution)/shard_map/mul | solution.py:23
  49.3 1.7 %mul.12 = f32[16,32,1024]{2,1,0:T(8,128)S(1)} reshape(f32[16,32,8,128]{3,2,1,0:T(8,128)} %mul.11) | data formatting | bytes 4194304 | tf_op jit(solution)/shard_map/mul | solution.py:23
  51.0 0.0 copy-start.2
  51.0 18.9 %all-to-all-done = bf16[32,16,1024]{2,0,1:T(8,128)(2,1)S(1)} async-done(((bf16[32,16,1024]{2,0,1:T(8,128)(2,1)}), bf16[32,16,1024]{2,0,1:T(8,128)(2,1)S(1)}, u32[]{:S(2)}, u32[]{:S(2)}) %all-to-all-start) | async-done | bytes 1048608 | tf_op jit(solution)/shard_map/all_to_all | solution.py:32
  69.9 0.0 copy-start.1
  69.9 0.3 fusion.1
  70.2 0.0 copy-done.2
  70.3 0.1 reduce_max.19
  70.4 0.1 copy.20
  70.5 0.1 copy.21
  70.6 0.1 div.25
  70.7 0.7 fusion.2
  71.4 0.0 all-gather.2.cloned.1.call-update
  71.4 22.6 %all_gather.7 = bf16[32,128]{0,1:T(8,128)(2,1)S(1)} all-gather(bf16[32,8]{0,1:T(8,128)(2,1)S(1)} %add_convert_fusion.1), channel_id=1, replica_groups=mesh['groups'=2,'tp'=16] {'tp'}, dimensions={1}, use_global_device_ids=true | all-gather | bytes 8704 | tf_op jit(solution)/shard_map/all_gather | solution.py:40
  94.0 0.7 copy.22
  94.7 17.0 %all-gather.2.cloned.1.call-done = bf16[32,16384]{1,0:T(8,128)(2,1)} async-done(((bf16[32,1024]{1,0:T(8,128)(2,1)}), bf16[32,16384]{1,0:T(8,128)(2,1)}) %all-gather.2.cloned.1.call-update) | async-done | bytes 1048592 | tf_op jit(solution)/shard_map/all_gather | solution.py:39
  111.7 2.3 %copy.33 = bf16[32,16384]{1,0:T(8,128)(2,1)} copy(bf16[32,16384]{1,0:T(8,128)(2,1)} %all-gather.2.cloned.1.call-done) | data formatting | bytes 2097152
  113.9 0.0 copy-done.1
  (6 shorter events, 0.1 us)
Async XLA Ops:
  7.2 0.9 copy-start
  29.7 13.7 %all-to-all-start.1 = ((bf16[16,2,128]{2,1,0:T(2,128)(2,1)}), bf16[16,2,128]{2,1,0:T(2,128)(2,1)S(1)}, u32[]{:S(2)}, u32[]{:S(2)}) async-start(bf16[16,2,128]{2,1,0:T(2,128)(2,1)} %reshape.42), calls=%async_computation.1 | async-start | bytes 16384 | tf_op jit(solution)/shard_map/all_to_all | solution.py:33
  43.4 26.6 %all-to-all-start = ((bf16[32,16,1024]{2,0,1:T(8,128)(2,1)}), bf16[32,16,1024]{2,0,1:T(8,128)(2,1)S(1)}, u32[]{:S(2)}, u32[]{:S(2)}) async-start(bf16[32,16,1024]{2,0,1:T(8,128)(2,1)} %bitcast.36), calls=%async_computation | async-start | bytes 2097152 | tf_op jit(solution)/shard_map/all_to_all | solution.py:32
  47.0 64.6 %all-gather.2.cloned.1.call-start = ((), (), s32[]{:S(2)}) async-start(), calls=%async_computation.2 | async-start | bytes 1114112 | tf_op jit(solution)/shard_map/all_gather | solution.py:39
  51.0 19.2 %copy-start.2 = (bf16[32,1024]{1,0:T(8,128)(2,1)S(1)}, bf16[32,1024]{1,0:T(8,128)(2,1)}, u32[]{:S(2)}) copy-start(bf16[32,1024]{1,0:T(8,128)(2,1)} %param.5) | copy-start | bytes 196612
  69.9 44.0 %copy-start.1 = (bf16[32,1664]{1,0:T(8,128)(2,1)S(1)}, bf16[32,1664]{1,0:T(8,128)(2,1)}, u32[]{:S(2)}) copy-start(bf16[32,1664]{1,0:T(8,128)(2,1)} %param.3) | copy-start | bytes 319492
Sparse Core Ops, SparseCore 0:
  71.5 40.1 all-gather.1
where the time goes:
time: 121 us
  waiting for transfers between devices  39.3 us (32%)
  blocking collectives  22.6 us (19%)
  matrix products  19.6 us (16%)
  between operations  14.2 us (12%)
  starting transfers between devices  11.1 us (9%)
  local copies, waits for them, and re-layouts  10.8 us (9%)
  other arithmetic  3.22 us (3%)
    all_gather x1, blocking collectives, shards(): lax.all_gather(local_scales, 'tp', axis=1, tiled=True)  22.6 us
    dot_general x1, matrix products, shards(): term = jnp.dot(hidden, down_weight, preferred_element_type=jnp.float32)  19.6 us
    all_to_all x1, waiting for transfers between devices, shards(): lax.all_to_all(coded, 'tp', split_axis=1, concat_axis=0, tiled=True)  18.9 us
    all_gather x1, waiting for transfers between devices, shards(): lax.all_gather(local_values, 'tp', axis=1, tiled=True)  17 us
    all_to_all x1, starting transfers between devices, shards(): lax.all_to_all(scale, 'tp', split_axis=1, concat_axis=0, tiled=True)  7.36 us
    unnamed x13, local copies, waits for them, and re-layouts  5.03 us
    mul x2, local copies, waits for them, and re-layouts, decode_sum(): return jnp.sum(blocks * factors, axis=0).reshape(row_count, width)  3.67 us
    all_to_all x1, starting transfers between devices, shards(): lax.all_to_all(coded, 'tp', split_axis=1, concat_axis=0, tiled=True)  3.66 us
  transfers between devices with their start and end apart: 3, of which 3 were waited for; matrix products, arithmetic and copies ran while one was open for 6% of the time, Pallas kernels for 0%

commit v1 on v0

v1 whole, which is shorter than its diff:
```python
import functools

import jax
import jax.numpy as jnp
from jax import lax
from jax.experimental import pallas as pl
from jax.experimental.pallas import tpu as pltpu
from jax.sharding import PartitionSpec as P

BLOCK = 128
MESH = pl.DeviceIdType.MESH
BF16 = jnp.bfloat16
F32 = jnp.float32
SLOTS = 16


def factor(count):
    chips = count // 2
    x = 1 << ((chips.bit_length() - 1) // 3)
    return chips // x, x


def kernel(
    n, h_hbm, w_hbm, res_ref, out_ref, osc_ref,
    h_ref, wbuf, a_send, a_recv, a_acc, b_send, b_recv, b_acc, c_send, c_recv, c_acc,
    g_ref, sc_acc, sz, sx, sk, h_sem, w_sem,
    sa, ra, sb, rb, sc, rc, sgz, rgz, sgx, rgx, sgk, rgk, ssz, rsz, ssx, rsx, ssk, rsk,
):
    zs, xs = factor(n)
    half = zs * xs
    chunks = g_ref.shape[0]
    rows, w = g_ref.shape[4], g_ref.shape[5]
    cols = chunks * w
    total = chunks * n
    slots = wbuf.shape[0]
    me = lax.axis_index("tp")
    mk, mx, mz = lax.rem(me, 2), lax.rem(me // 2, xs), me // (2 * xs)

    def device(z, x, k):
        return {"tp": (z * xs + x) * 2 + k}

    core_peer = device(mz, mx, 1 - mk)

    def x_peer(j):
        return lax.rem(mx + j + xs, xs)

    def z_peer(j):
        return lax.rem(mz + j + zs, zs)

    def w_copy(g):
        chunk, p = g // n, lax.rem(g, n)
        k = lax.rem(mk + 1 + p // half, 2)
        r = lax.rem(p, half)
        x, z = r // zs, lax.rem(r, zs)
        column = pl.multiple_of(((z * xs + x) * 2 + k) * cols + chunk * w, 128)
        slot = lax.rem(g, slots)
        return pltpu.make_async_copy(w_hbm.at[:, pl.ds(column, w)], wbuf.at[slot], w_sem.at[slot])

    def remote(src, dst, send, recv, dev):
        return pltpu.make_async_remote_copy(
            src_ref=src, dst_ref=dst, send_sem=send, recv_sem=recv, device_id=dev, device_id_type=MESH
        )

    h_copy = pltpu.make_async_copy(h_hbm, h_ref, h_sem)
    h_copy.start()

    def prime(g, carry):
        w_copy(g).start()
        return carry

    lax.fori_loop(0, min(slots, total), prime, 0)

    barrier = pltpu.get_barrier_semaphore()
    peers = [core_peer]
    peers += [device(mz, x_peer(j), mk) for j in range(1, xs)]
    peers += [device(z_peer(j), mx, mk) for j in range(1, zs)]
    for peer in peers:
        pl.semaphore_signal(barrier, inc=1, device_id=peer, device_id_type=MESH)
    sc_acc[...] = jnp.zeros_like(sc_acc)
    h_copy.wait()

    def multiply(c, start, stop, store):
        def body(p, carry):
            g = c * n + p
            w_copy(g).wait()
            term = jnp.dot(h_ref[...], wbuf[lax.rem(g, slots)], preferred_element_type=F32)
            store(lax.rem(p, half), term)

            @pl.when(g + slots < total)
            def _():
                w_copy(g + slots).start()

            return carry

        lax.fori_loop(start, stop, body, 0)

    def to_send(c):
        def store(r, term):
            a_send[c, r // zs, lax.rem(r, zs)] = term.astype(BF16)

        return store

    def to_keep(c):
        def store(r, term):
            a_acc[r // zs, lax.rem(r, zs)] = term

        return store

    def core_copy(c):
        return remote(a_send.at[c], a_recv.at[c], sa.at[c], ra.at[c], core_peer)

    def x_copy(c, j):
        return remote(b_send.at[c, j - 1], b_recv.at[c, j - 1], sb.at[c, j - 1], rb.at[c, j - 1], device(mz, x_peer(j), mk))

    def z_copy(c, j):
        return remote(c_send.at[c, j - 1], c_recv.at[c, j - 1], sc.at[c, j - 1], rc.at[c, j - 1], device(z_peer(j), mx, mk))

    def gz_copy(c, j, z):
        part = g_ref.at[c, mk, mx, z]
        return remote(part, part, sgz.at[c, j - 1], rgz.at[c, j - 1], device(z_peer(j), mx, mk))

    def gx_copy(c, j, x):
        part = g_ref.at[c, mk, x]
        return remote(part, part, sgx.at[c, j - 1], rgx.at[c, j - 1], device(mz, x_peer(j), mk))

    def gk_copy(c, k):
        part = g_ref.at[c, k]
        return remote(part, part, sgk.at[c], rgk.at[c], core_peer)

    def sz_copy(j):
        return remote(sz.at[0], sz.at[j], ssz.at[j - 1], rsz.at[j - 1], device(z_peer(j), mx, mk))

    def sx_copy(j):
        return remote(sx.at[0], sx.at[j], ssx.at[j - 1], rsx.at[j - 1], device(mz, x_peer(j), mk))

    def sk_copy():
        return remote(sk.at[0], sk.at[1], ssk, rsk, core_peer)

    def gathered(buf, count):
        value = buf[0].astype(F32)
        for j in range(1, count):
            value = value + buf[j].astype(F32)
        return value.astype(BF16)

    def reduce_core(c):
        core_copy(c).wait_recv()
        for j in range(1, xs):
            x = x_peer(j)
            b_send[c, j - 1] = (a_acc[x] + a_recv[c, x].astype(F32)).astype(BF16)
            x_copy(c, j).start()
        b_acc[c] = a_acc[mx] + a_recv[c, mx].astype(F32)

    def reduce_x(c):
        for j in range(1, xs):
            x_copy(c, j).wait_recv()

        def part(z):
            value = b_acc[c, z]
            for j in range(1, xs):
                value = value + b_recv[c, j - 1, z].astype(F32)
            return value

        for j in range(1, zs):
            c_send[c, j - 1] = part(z_peer(j)).astype(BF16)
            z_copy(c, j).start()
        c_acc[c] = part(mz) + res_ref[:, c * w:(c + 1) * w].astype(F32)

    def reduce_z(c):
        for j in range(1, zs):
            z_copy(c, j).wait_recv()
        summed = c_acc[c]
        for j in range(1, zs):
            summed = summed + c_recv[c, j - 1].astype(F32)
        lane = lax.broadcasted_iota(jnp.int32, sc_acc.shape, 1)
        first = (me * cols + c * w) // BLOCK
        for b in range(w // BLOCK):
            block = summed[:, b * BLOCK:(b + 1) * BLOCK]
            scale = (jnp.max(jnp.abs(block), axis=1, keepdims=True) + 1e-6).astype(BF16).astype(F32)
            g_ref[c, mk, mx, mz, :, b * BLOCK:(b + 1) * BLOCK] = (block / scale).astype(BF16)
            sc_acc[...] = jnp.where(lane == first + b, scale, sc_acc[...])
        for j in range(1, zs):
            gz_copy(c, j, mz).start()
        if c == chunks - 1:
            sz[0] = sc_acc[...].astype(BF16)
            for j in range(1, zs):
                sz_copy(j).start()

    def gather_x(c):
        for j in range(1, zs):
            gz_copy(c, j, z_peer(-j)).wait_recv()
        for j in range(1, xs):
            gx_copy(c, j, mx).start()
        if c == chunks - 1:
            for j in range(1, zs):
                sz_copy(j).wait_recv()
            sx[0] = gathered(sz, zs)
            for j in range(1, xs):
                sx_copy(j).start()

    def gather_core(c):
        for j in range(1, xs):
            gx_copy(c, j, x_peer(-j)).wait_recv()
        gk_copy(c, mk).start()
        if c == chunks - 1:
            for j in range(1, xs):
                sx_copy(j).wait_recv()
            sk[0] = gathered(sx, xs)
            sk_copy().start()

    def finish(c):
        gk_copy(c, 1 - mk).wait_recv()
        for k in range(2):
            for x in range(xs):
                for z in range(zs):
                    column = ((z * xs + x) * 2 + k) * cols + c * w
                    out_ref[:, column:column + w] = g_ref[c, k, x, z]
        if c == chunks - 1:
            sk_copy().wait_recv()
            osc_ref[...] = gathered(sk, 2)

    quarter = half // 2
    later = [[] for _ in range(4 * chunks + 16)]
    steps = ((0, reduce_core), (2, reduce_x), (4, reduce_z), (6, gather_x), (8, gather_core), (10, finish))
    for c in range(chunks):
        for delay, step in steps:
            later[4 * c + 3 + delay].append((step, c))
    for t in range(4 * chunks + 16):
        if t < 4 * chunks:
            c, q = t // 4, t % 4
            multiply(c, q * quarter, (q + 1) * quarter, to_send(c) if q < 2 else to_keep(c))
            if q == 1:
                if c == 0:
                    pl.semaphore_wait(barrier, len(peers))
                core_copy(c).start()
        for step, c in later[t]:
            step(c)

    for c in range(chunks):
        core_copy(c).wait_send()
        gk_copy(c, mk).wait_send()
        for j in range(1, xs):
            x_copy(c, j).wait_send()
            gx_copy(c, j, mx).wait_send()
        for j in range(1, zs):
            z_copy(c, j).wait_send()
            gz_copy(c, j, mz).wait_send()
    for j in range(1, zs):
        sz_copy(j).wait_send()
    for j in range(1, xs):
        sx_copy(j).wait_send()
    sk_copy().wait_send()


def shards(hidden, down_weight, residual):
    n = lax.axis_size("tp")
    zs, xs = factor(n)
    rows, depth = hidden.shape
    width = down_weight.shape[1]
    cols = width // n
    w = min(256, cols)
    chunks = cols // w
    dma = pltpu.SemaphoreType.DMA
    vmem = pltpu.VMEM
    scratch = [
        vmem((rows, depth), BF16),
        vmem((SLOTS, depth, w), BF16),
        vmem((chunks, xs, zs, rows, w), BF16),
        vmem((chunks, xs, zs, rows, w), BF16),
        vmem((xs, zs, rows, w), F32),
        vmem((chunks, xs - 1, zs, rows, w), BF16),
        vmem((chunks, xs - 1, zs, rows, w), BF16),
        vmem((chunks, zs, rows, w), F32),
        vmem((chunks, zs - 1, rows, w), BF16),
        vmem((chunks, zs - 1, rows, w), BF16),
        vmem((chunks, rows, w), F32),
        vmem((chunks, 2, xs, zs, rows, w), BF16),
        vmem((rows, width // BLOCK), F32),
        vmem((zs, rows, width // BLOCK), BF16),
        vmem((xs, rows, width // BLOCK), BF16),
        vmem((2, rows, width // BLOCK), BF16),
        dma, dma((SLOTS,)),
        dma((chunks,)), dma((chunks,)),
        dma((chunks, xs - 1)), dma((chunks, xs - 1)),
        dma((chunks, zs - 1)), dma((chunks, zs - 1)),
        dma((chunks, zs - 1)), dma((chunks, zs - 1)),
        dma((chunks, xs - 1)), dma((chunks, xs - 1)),
        dma((chunks,)), dma((chunks,)),
        dma((zs - 1,)), dma((zs - 1,)),
        dma((xs - 1,)), dma((xs - 1,)),
        dma, dma,
    ]
    hbm = pl.BlockSpec(memory_space=pl.ANY)
    whole = pl.BlockSpec(memory_space=pltpu.VMEM)
    return pl.pallas_call(
        functools.partial(kernel, n),
        out_shape=(
            jax.ShapeDtypeStruct((rows, width), BF16),
            jax.ShapeDtypeStruct((rows, width // BLOCK), BF16),
        ),
        in_specs=[hbm, hbm, whole],
        out_specs=(whole, whole),
        scratch_shapes=scratch,
        compiler_params=pltpu.CompilerParams(collective_id=0, has_side_effects=True, vmem_limit_bytes=48 * 2**20),
        cost_estimate=pl.CostEstimate(
            flops=2 * rows * depth * width, bytes_accessed=2 * depth * width, transcendentals=0
        ),
    )(hidden, down_weight, residual)


def solution(mesh):
    in_specs = (P("groups", "tp"), P("tp", None), P("groups", "tp"))
    out_specs = (P("groups", None), P("groups", None))
    return jax.shard_map(shards, mesh=mesh, in_specs=in_specs, out_specs=out_specs, check_vma=False)
```

time: 121 us -> 53.1 us (0.44)
  Pallas kernels: 0 us -> 49 us
  waiting for transfers between devices: 39.3 us -> 0 us
  blocking collectives: 22.6 us -> 0 us
  matrix products: 19.6 us -> 0 us
  between operations: 14.2 us -> 0.65 us
  starting transfers between devices: 11.1 us -> 0 us
  local copies, waits for them, and re-layouts: 10.8 us -> 3.3 us
  other arithmetic: 3.22 us -> 0 us
    pallas_call x0 -> x1, Pallas kernels: none -> 49 us  [shards(): pl.pallas_call(functools.partial(kernel, n), out_shape=(jax.ShapeDtypeStr...]
    all_gather x1 -> x0, blocking collectives: 22.6 us -> none  [shards(): lax.all_gather(local_scales, 'tp', axis=1, tiled=True)]
    all_to_all x2 -> x0, waiting for transfers between devices: 22.3 us -> none  [the longest x1 18.9 us: shards(): lax.all_to_all(coded, 'tp', split_axis=1, concat_axis=0, tiled=True)]
    dot_general x1 -> x0, matrix products: 19.6 us -> none  [shards(): term = jnp.dot(hidden, down_weight, preferred_element_type=jnp.float32)]
    all_gather x1 -> x0, waiting for transfers between devices: 17 us -> none  [shards(): lax.all_gather(local_values, 'tp', axis=1, tiled=True)]
    all_to_all x2 -> x0, starting transfers between devices: 11 us -> none  [the longest x1 7.36 us: shards(): lax.all_to_all(scale, 'tp', split_axis=1, concat_axis=0, tiled=True)]
    mul x2 -> x0, local copies, waits for them, and re-layouts: 3.67 us -> none  [decode_sum(): return jnp.sum(blocks * factors, axis=0).reshape(row_count, width)]
    convert_element_type x5 -> x0, other arithmetic: 2 us -> none  [the longest x2 1.98 us: encode(): (blocks / scale.astype(jnp.float32)[:, :, None]).astype(jnp.bfloat16)]
  transfers between devices with their start and end apart: 3 -> 0, of which waited for: 3 -> 0; matrix products, arithmetic and copies ran while one was open for 6% -> 0% of each run, Pallas kernels for 0% -> 0%
where the time goes in v1:
time: 53.1 us; the launch traced here: 53 us
  Pallas kernels  49 us (92%)
  local copies, waits for them, and re-layouts  3.3 us (6%)
  between operations  0.65 us (1%)
    pallas_call x1, Pallas kernels, shards(): pl.pallas_call(functools.partial(kernel, n), out_shape=(jax.ShapeDtypeStr...  49 us
    unnamed x6, local copies, waits for them, and re-layouts  3.3 us

profile of v1, /device:TPU:0, one launch (start us, length us, event | category | flops | bytes accessed | tf_op | source)
XLA Modules:
  0.0 53.0 jit_solution(16286747829856723812)
XLA Ops:
  0.6 0.0 copy-start
  0.6 0.9 %copy-done = bf16[32,1664]{1,0:T(8,128)(2,1)S(1)} copy-done((bf16[32,1664]{1,0:T(8,128)(2,1)S(1)}, bf16[32,1664]{1,0:T(8,128)(2,1)}, u32[]{:S(2)}) %copy-start) | copy-done | bytes 106520
  1.5 0.0 copy-start.1
  1.5 0.8 %copy-done.1 = bf16[32,1024]{1,0:T(8,128)(2,1)S(1)} copy-done((bf16[32,1024]{1,0:T(8,128)(2,1)S(1)}, bf16[32,1024]{1,0:T(8,128)(2,1)}, u32[]{:S(2)}) %copy-start.1) | copy-done | bytes 65560
  2.4 49.0 %shard_map.50 = (bf16[32,16384]{1,0:T(8,128)(2,1)S(1)}, bf16[32,128]{1,0:T(8,128)(2,1)S(1)}) custom-call(bf16[32,1664]{1,0:T(8,128)(2,1)S(1)} %copy-done, bf16[1664,16384]{1,0:T(8,128)(2,1)} %w_hbm.1, bf16[32,1024]{1,0:T(8,128)(2,1)S(1)} %copy-done.1), custom_call_target="tpu_custom_call" | custom-call | flops 1744830464 | bytes 54525952 | tf_op jit(solution)/shard_map/pallas_call | solution.py:294
  51.4 1.0 %copy.7 = bf16[32,16384]{1,0:T(8,128)(2,1)} copy(bf16[32,16384]{1,0:T(8,128)(2,1)S(1)} %get-tuple-element.4) | data formatting | bytes 2097152
  52.4 0.6 %copy.8 = bf16[32,128]{1,0:T(8,128)(2,1)} copy(bf16[32,128]{1,0:T(8,128)(2,1)S(1)} %get-tuple-element.5) | data formatting | bytes 16384
Async XLA Ops:
  0.6 0.9 %copy-start = (bf16[32,1664]{1,0:T(8,128)(2,1)S(1)}, bf16[32,1664]{1,0:T(8,128)(2,1)}, u32[]{:S(2)}) copy-start(bf16[32,1664]{1,0:T(8,128)(2,1)} %h_hbm.1) | copy-start | bytes 319492
  1.5 0.8 %copy-start.1 = (bf16[32,1024]{1,0:T(8,128)(2,1)S(1)}, bf16[32,1024]{1,0:T(8,128)(2,1)}, u32[]{:S(2)}) copy-start(bf16[32,1024]{1,0:T(8,128)(2,1)} %res_ref.1) | copy-start | bytes 196612

commit v2 on v1

v2 whole, which is shorter than its diff:
```python
import functools

import jax
import jax.numpy as jnp
from jax import lax
from jax.experimental import pallas as pl
from jax.experimental.pallas import tpu as pltpu
from jax.sharding import PartitionSpec as P

BLOCK = 128
MESH = pl.DeviceIdType.MESH
BF16 = jnp.bfloat16
F32 = jnp.float32
SLOTS = 16
DIRECT = 2
WIDE_DELAYS = (0, 3, 6, 9, 12, 13)
NARROW_DELAYS = (0, 3.6, 7.2, 8.2)


def factor(count):
    chips = count // 2
    x = 1 << ((chips.bit_length() - 1) // 3)
    return chips // x, x


def plan(cols, n):
    narrow = DIRECT if cols >= 4 * BLOCK and n <= 32 else 0
    wide = min(2 * BLOCK, cols)
    return (cols - narrow * BLOCK) // wide, wide, narrow


class Refs:
    def __init__(self, names, refs):
        for name, ref in zip(names, refs):
            setattr(self, name, ref)


def kernel(n, names, h_hbm, w_hbm, res_ref, out_ref, osc_ref, *scratch):
    s = Refs(names, scratch)
    zs, xs = factor(n)
    half = zs * xs
    rows, cols = res_ref.shape
    wides, wide, narrows = plan(cols, n)
    chunks = wides + narrows
    slot_w = s.wbuf.shape[2]
    per_wide = slot_w // wide
    wide_items = wides * n // per_wide
    total = wide_items + narrows * n * BLOCK // slot_w
    slots = s.wbuf.shape[0]
    me = lax.axis_index("tp")
    mk, mx, mz = lax.rem(me, 2), lax.rem(me // 2, xs), me // (2 * xs)
    chip = me // 2

    def device(z, x, k):
        return {"tp": (z * xs + x) * 2 + k}

    core_peer = device(mz, mx, 1 - mk)

    def x_peer(j):
        return lax.rem(mx + j + xs, xs)

    def z_peer(j):
        return lax.rem(mz + j + zs, zs)

    def chip_peer(j):
        return lax.rem(chip + j + half, half)

    def item_copies(g, first, offset, w):
        pieces = slot_w // w
        items = n // pieces
        chunk, p = (g - first) // items, lax.rem(g - first, items)
        k = lax.rem(mk + 1 + p // (items // 2), 2)
        r = lax.rem(p, items // 2) * pieces
        x, z = r // zs, lax.rem(r, zs)
        slot = lax.rem(g, slots)
        copies = []
        for i in range(pieces):
            column = pl.multiple_of(((((z + i) * xs + x) * 2 + k) * cols + offset) + chunk * w, BLOCK)
            copies.append(
                pltpu.make_async_copy(
                    w_hbm.at[:, pl.ds(column, w)], s.wbuf.at[slot, :, pl.ds(i * w, w)], s.w_sem.at[slot, i]
                )
            )
        return copies

    def wide_copies(g):
        return item_copies(g, 0, 0, wide)

    def narrow_copies(g):
        return item_copies(g, wide_items, wides * wide, BLOCK)

    def start_item(g):
        @pl.when(g < wide_items)
        def _():
            for copy in wide_copies(g):
                copy.start()

        if narrows:
            @pl.when(jnp.logical_and(g >= wide_items, g < total))
            def _():
                for copy in narrow_copies(g):
                    copy.start()

    def remote(src, dst, send, recv, dev):
        return pltpu.make_async_remote_copy(
            src_ref=src, dst_ref=dst, send_sem=send, recv_sem=recv, device_id=dev, device_id_type=MESH
        )

    h_copy = pltpu.make_async_copy(h_hbm, s.h, s.h_sem)
    h_copy.start()

    def prime(g, carry):
        start_item(g)
        return carry

    lax.fori_loop(0, min(slots, total), prime, 0)

    barrier = pltpu.get_barrier_semaphore()
    peers = [core_peer]
    if narrows:
        peers += [{"tp": chip_peer(j) * 2 + mk} for j in range(1, half)]
    else:
        peers += [device(mz, x_peer(j), mk) for j in range(1, xs)]
        peers += [device(z_peer(j), mx, mk) for j in range(1, zs)]
    for peer in peers:
        pl.semaphore_signal(barrier, inc=1, device_id=peer, device_id_type=MESH)
    s.sc_acc[...] = jnp.zeros_like(s.sc_acc)
    h_copy.wait()

    def multiply(first, start, stop, copies, store):
        def body(p, carry):
            g = first + p
            for copy in copies(g):
                copy.wait()
            term = jnp.dot(s.h[...], s.wbuf[lax.rem(g, slots)], preferred_element_type=F32)
            store(p, term)
            start_item(g + slots)
            return carry

        lax.fori_loop(start, stop, body, 0, unroll=min(4, stop - start))

    def storing(ref, w, kind):
        pieces = slot_w // w
        items = n // pieces // 2

        def store(p, term):
            r = lax.rem(p, items) * pieces
            for i in range(pieces):
                ref[r // zs, lax.rem(r, zs) + i] = term[:, i * w:(i + 1) * w].astype(kind)

        return store

    def core_copy(c):
        return remote(s.a_send.at[c], s.a_recv.at[c], s.sa.at[c], s.ra.at[c], core_peer)

    def x_copy(c, j):
        return remote(s.b_send.at[c, j - 1], s.b_recv.at[c, j - 1], s.sb.at[c, j - 1], s.rb.at[c, j - 1], device(mz, x_peer(j), mk))

    def z_copy(c, j):
        return remote(s.c_send.at[c, j - 1], s.c_recv.at[c, j - 1], s.sc.at[c, j - 1], s.rc.at[c, j - 1], device(z_peer(j), mx, mk))

    def gz_copy(c, j, z):
        part = s.g.at[c, mk, mx, z]
        return remote(part, part, s.sgz.at[c, j - 1], s.rgz.at[c, j - 1], device(z_peer(j), mx, mk))

    def gx_copy(c, j, x):
        part = s.g.at[c, mk, x]
        return remote(part, part, s.sgx.at[c, j - 1], s.rgx.at[c, j - 1], device(mz, x_peer(j), mk))

    def gk_copy(c, k):
        part = s.g.at[c, k]
        return remote(part, part, s.sgk.at[c], s.rgk.at[c], core_peer)

    def d_core_copy(c):
        return remote(s.e_send.at[c], s.e_recv.at[c], s.se.at[c], s.re.at[c], core_peer)

    def d_copy(c, j):
        return remote(s.d_send.at[c, j - 1], s.d_recv.at[c, j - 1], s.sd.at[c, j - 1], s.rd.at[c, j - 1], {"tp": chip_peer(j) * 2 + mk})

    def dg_copy(c, j, owner):
        part = s.dg.at[c, mk, lax.rem(owner, xs), owner // xs]
        return remote(part, part, s.sdg.at[c, j - 1], s.rdg.at[c, j - 1], {"tp": chip_peer(j) * 2 + mk})

    def dgk_copy(c, k):
        part = s.dg.at[c, k]
        return remote(part, part, s.sdk.at[c], s.rdk.at[c], core_peer)

    def sz_copy(j):
        return remote(s.sz.at[0], s.sz.at[j], s.ssz.at[j - 1], s.rsz.at[j - 1], device(z_peer(j), mx, mk))

    def sx_copy(j):
        return remote(s.sx.at[0], s.sx.at[j], s.ssx.at[j - 1], s.rsx.at[j - 1], device(mz, x_peer(j), mk))

    def sd_copy(j):
        return remote(s.sd_buf.at[0], s.sd_buf.at[j], s.ssd.at[j - 1], s.rsd.at[j - 1], {"tp": chip_peer(j) * 2 + mk})

    def sk_copy():
        return remote(s.sk.at[0], s.sk.at[1], s.ssk, s.rsk, core_peer)

    def gathered(buf, count):
        value = buf[0].astype(F32)
        for j in range(1, count):
            value = value + buf[j].astype(F32)
        return value.astype(BF16)

    def encode(summed, offset, out):
        lane = lax.broadcasted_iota(jnp.int32, s.sc_acc.shape, 1)
        first = (me * cols + offset) // BLOCK
        for b in range(summed.shape[1] // BLOCK):
            block = summed[:, b * BLOCK:(b + 1) * BLOCK]
            scale = (jnp.max(jnp.abs(block), axis=1, keepdims=True) + 1e-6).astype(BF16).astype(F32)
            out[:, b * BLOCK:(b + 1) * BLOCK] = (block / scale).astype(BF16)
            s.sc_acc[...] = jnp.where(lane == first + b, scale, s.sc_acc[...])

    def write_out(part, k, offset, w):
        for x in range(xs):
            for z in range(zs):
                column = ((z * xs + x) * 2 + k) * cols + offset
                out_ref[:, column:column + w] = part[k, x, z]

    def reduce_core(c):
        core_copy(c).wait_recv()
        for j in range(1, xs):
            x = x_peer(j)
            s.b_send[c, j - 1] = (s.a_acc[x] + s.a_recv[c, x].astype(F32)).astype(BF16)
            x_copy(c, j).start()
        s.b_acc[c] = s.a_acc[mx] + s.a_recv[c, mx].astype(F32)

    def reduce_x(c):
        for j in range(1, xs):
            x_copy(c, j).wait_recv()

        def part(z):
            value = s.b_acc[c, z]
            for j in range(1, xs):
                value = value + s.b_recv[c, j - 1, z].astype(F32)
            return value

        for j in range(1, zs):
            s.c_send[c, j - 1] = part(z_peer(j)).astype(BF16)
            z_copy(c, j).start()
        s.c_acc[c] = part(mz) + res_ref[:, c * wide:(c + 1) * wide].astype(F32)

    def reduce_z(c):
        for j in range(1, zs):
            z_copy(c, j).wait_recv()
        summed = s.c_acc[c]
        for j in range(1, zs):
            summed = summed + s.c_recv[c, j - 1].astype(F32)
        encode(summed, c * wide, s.g.at[c, mk, mx, mz])
        for j in range(1, zs):
            gz_copy(c, j, mz).start()
        if c == chunks - 1:
            s.sz[0] = s.sc_acc[...].astype(BF16)
            for j in range(1, zs):
                sz_copy(j).start()

    def gather_x(c):
        for j in range(1, zs):
            gz_copy(c, j, z_peer(-j)).wait_recv()
        for j in range(1, xs):
            gx_copy(c, j, mx).start()
        if c == chunks - 1:
            for j in range(1, zs):
                sz_copy(j).wait_recv()
            s.sx[0] = gathered(s.sz, zs)
            for j in range(1, xs):
                sx_copy(j).start()

    def gather_core(c):
        for j in range(1, xs):
            gx_copy(c, j, x_peer(-j)).wait_recv()
        gk_copy(c, mk).start()
        if c == chunks - 1:
            for j in range(1, xs):
                sx_copy(j).wait_recv()
            s.sk[0] = gathered(s.sx, xs)
            sk_copy().start()

    def finish(c):
        gk_copy(c, 1 - mk).wait_recv()
        for k in range(2):
            write_out(s.g.at[c], k, c * wide, wide)
        if c == chunks - 1:
            sk_copy().wait_recv()
            osc_ref[...] = gathered(s.sk, 2)

    def narrow_at(c):
        return wides * wide + c * BLOCK

    def d_reduce_core(c):
        d_core_copy(c).wait_recv()
        for j in range(1, half):
            q = chip_peer(j)
            x, z = lax.rem(q, xs), q // xs
            s.d_send[c, j - 1] = (s.e_acc[x, z] + s.e_recv[c, x, z].astype(F32)).astype(BF16)
            d_copy(c, j).start()
        at = narrow_at(c)
        s.d_acc[c] = s.e_acc[mx, mz] + s.e_recv[c, mx, mz].astype(F32) + res_ref[:, at:at + BLOCK].astype(F32)

    def d_reduce(c):
        for j in range(1, half):
            d_copy(c, j).wait_recv()
        summed = s.d_acc[c]
        for j in range(1, half):
            summed = summed + s.d_recv[c, j - 1].astype(F32)
        encode(summed, narrow_at(c), s.dg.at[c, mk, mx, mz])
        for j in range(1, half):
            dg_copy(c, j, chip).start()
        if c == narrows - 1:
            s.sd_buf[0] = s.sc_acc[...].astype(BF16)
            for j in range(1, half):
                sd_copy(j).start()

    def d_gather_core(c):
        for j in range(1, half):
            dg_copy(c, j, chip_peer(-j)).wait_recv()
        dgk_copy(c, mk).start()
        if c == narrows - 1:
            for j in range(1, half):
                sd_copy(j).wait_recv()
            s.sk[0] = gathered(s.sd_buf, half)
            sk_copy().start()

    def d_finish(c):
        dgk_copy(c, 1 - mk).wait_recv()
        for k in range(2):
            write_out(s.dg.at[c], k, narrow_at(c), BLOCK)
        if c == narrows - 1:
            sk_copy().wait_recv()
            osc_ref[...] = gathered(s.sk, 2)

    line = []

    def matmul_unit(first, start, stop, copies, store):
        return lambda: multiply(first, start, stop, copies, store)

    def send_core(copy, c, opening):
        def step():
            if opening:
                pl.semaphore_wait(barrier, len(peers))
            copy(c).start()

        return step

    for c in range(wides):
        items = n // per_wide
        for q in range(4):
            store = storing(s.a_send.at[c], wide, BF16) if q < 2 else storing(s.a_acc, wide, F32)
            unit = matmul_unit(c * items, q * items // 4, (q + 1) * items // 4, wide_copies, store)
            line.append((4 * c + q, 0, unit))
        line.append((4 * c + 1, 1, send_core(core_copy, c, c == 0)))
        for order, (delay, step) in enumerate(zip(WIDE_DELAYS, (reduce_core, reduce_x, reduce_z, gather_x, gather_core, finish))):
            line.append((4 * c + 3 + delay, 2 + order, functools.partial(step, c)))
    for c in range(narrows):
        items = n * BLOCK // slot_w
        for q in range(2):
            store = storing(s.e_send.at[c], BLOCK, BF16) if q < 1 else storing(s.e_acc, BLOCK, F32)
            unit = matmul_unit(wide_items + c * items, q * items // 2, (q + 1) * items // 2, narrow_copies, store)
            line.append((4 * wides + 2 * c + q, 0, unit))
        line.append((4 * wides + 2 * c, 1, send_core(d_core_copy, c, False)))
        for order, (delay, step) in enumerate(zip(NARROW_DELAYS, (d_reduce_core, d_reduce, d_gather_core, d_finish))):
            line.append((4 * wides + 2 * c + 1 + delay, 2 + order, functools.partial(step, c)))
    for time, order, step in sorted(line, key=lambda entry: entry[:2]):
        step()

    for c in range(wides):
        core_copy(c).wait_send()
        gk_copy(c, mk).wait_send()
        for j in range(1, xs):
            x_copy(c, j).wait_send()
            gx_copy(c, j, mx).wait_send()
        for j in range(1, zs):
            z_copy(c, j).wait_send()
            gz_copy(c, j, mz).wait_send()
    for c in range(narrows):
        d_core_copy(c).wait_send()
        dgk_copy(c, mk).wait_send()
        for j in range(1, half):
            d_copy(c, j).wait_send()
            dg_copy(c, j, chip).wait_send()
    if narrows:
        for j in range(1, half):
            sd_copy(j).wait_send()
    else:
        for j in range(1, zs):
            sz_copy(j).wait_send()
        for j in range(1, xs):
            sx_copy(j).wait_send()
    sk_copy().wait_send()


def shards(hidden, down_weight, residual):
    n = lax.axis_size("tp")
    zs, xs = factor(n)
    half = zs * xs
    rows, depth = hidden.shape
    width = down_weight.shape[1]
    cols = width // n
    wides, w, narrows = plan(cols, n)
    dma = pltpu.SemaphoreType.DMA
    vmem = pltpu.VMEM
    scales = (rows, width // BLOCK)
    scratch = {
        "h": vmem((rows, depth), BF16),
        "h_sem": dma,
        "wbuf": vmem((SLOTS, depth, 2 * BLOCK), BF16),
        "w_sem": dma((SLOTS, 2)),
        "a_send": vmem((wides, xs, zs, rows, w), BF16),
        "a_recv": vmem((wides, xs, zs, rows, w), BF16),
        "a_acc": vmem((xs, zs, rows, w), F32),
        "b_send": vmem((wides, xs - 1, zs, rows, w), BF16),
        "b_recv": vmem((wides, xs - 1, zs, rows, w), BF16),
        "b_acc": vmem((wides, zs, rows, w), F32),
        "c_send": vmem((wides, zs - 1, rows, w), BF16),
        "c_recv": vmem((wides, zs - 1, rows, w), BF16),
        "c_acc": vmem((wides, rows, w), F32),
        "g": vmem((wides, 2, xs, zs, rows, w), BF16),
        "sc_acc": vmem(scales, F32),
        "sk": vmem((2,) + scales, BF16),
        "ssk": dma,
        "rsk": dma,
    }
    for name, shape in (("a", ()), ("b", (xs - 1,)), ("c", (zs - 1,)), ("gz", (zs - 1,)), ("gx", (xs - 1,)), ("gk", ())):
        scratch["s" + name] = dma((wides,) + shape)
        scratch["r" + name] = dma((wides,) + shape)
    if narrows:
        scratch.update({
            "e_send": vmem((narrows, xs, zs, rows, BLOCK), BF16),
            "e_recv": vmem((narrows, xs, zs, rows, BLOCK), BF16),
            "e_acc": vmem((xs, zs, rows, BLOCK), F32),
            "d_send": vmem((narrows, half - 1, rows, BLOCK), BF16),
            "d_recv": vmem((narrows, half - 1, rows, BLOCK), BF16),
            "d_acc": vmem((narrows, rows, BLOCK), F32),
            "dg": vmem((narrows, 2, xs, zs, rows, BLOCK), BF16),
            "sd_buf": vmem((half,) + scales, BF16),
            "ssd": dma((half - 1,)),
            "rsd": dma((half - 1,)),
        })
        for name, shape in (("e", ()), ("d", (half - 1,)), ("dg", (half - 1,)), ("dk", ())):
            scratch["s" + name] = dma((narrows,) + shape)
            scratch["r" + name] = dma((narrows,) + shape)
    else:
        scratch.update({
            "sz": vmem((zs,) + scales, BF16),
            "sx": vmem((xs,) + scales, BF16),
            "ssz": dma((zs - 1,)),
            "rsz": dma((zs - 1,)),
            "ssx": dma((xs - 1,)),
            "rsx": dma((xs - 1,)),
        })
    hbm = pl.BlockSpec(memory_space=pl.ANY)
    whole = pl.BlockSpec(memory_space=pltpu.VMEM)
    return pl.pallas_call(
        functools.partial(kernel, n, tuple(scratch)),
        out_shape=(
            jax.ShapeDtypeStruct((rows, width), BF16),
            jax.ShapeDtypeStruct(scales, BF16),
        ),
        in_specs=[hbm, hbm, whole],
        out_specs=(whole, whole),
        scratch_shapes=list(scratch.values()),
        compiler_params=pltpu.CompilerParams(collective_id=0, has_side_effects=True, vmem_limit_bytes=48 * 2**20),
        cost_estimate=pl.CostEstimate(
            flops=2 * rows * depth * width, bytes_accessed=2 * depth * width, transcendentals=0
        ),
    )(hidden, down_weight, residual)


def solution(mesh):
    in_specs = (P("groups", "tp"), P("tp", None), P("groups", "tp"))
    out_specs = (P("groups", None), P("groups", None))
    return jax.shard_map(shards, mesh=mesh, in_specs=in_specs, out_specs=out_specs, check_vma=False)
```

time: 53.1 us -> 45 us (0.85)
  Pallas kernels: 49 us -> 40.9 us
    pallas_call x1, Pallas kernels: 49 us -> 40.9 us  [shards(): pl.pallas_call(functools.partial(kernel, n, tuple(scratch)), out_shape=(j...]
where the time goes in v2:
time: 45 us; the launch traced here: 44.8 us
  Pallas kernels  40.9 us (91%)
  local copies, waits for them, and re-layouts  3.3 us (7%)
  between operations  0.65 us (1%)
    pallas_call x1, Pallas kernels, shards(): pl.pallas_call(functools.partial(kernel, n, tuple(scratch)), out_shape=(j...  40.9 us
    unnamed x6, local copies, waits for them, and re-layouts  3.3 us

profile of v2, /device:TPU:0, one launch (start us, length us, event | category | flops | bytes accessed | tf_op | source)
XLA Modules:
  0.0 44.8 jit_solution(8778708850298237569)
XLA Ops:
  0.6 0.0 copy-start
  0.6 0.9 %copy-done = bf16[32,1664]{1,0:T(8,128)(2,1)S(1)} copy-done((bf16[32,1664]{1,0:T(8,128)(2,1)S(1)}, bf16[32,1664]{1,0:T(8,128)(2,1)}, u32[]{:S(2)}) %copy-start) | copy-done | bytes 106520
  1.5 0.0 copy-start.1
  1.5 0.8 %copy-done.1 = bf16[32,1024]{1,0:T(8,128)(2,1)S(1)} copy-done((bf16[32,1024]{1,0:T(8,128)(2,1)S(1)}, bf16[32,1024]{1,0:T(8,128)(2,1)}, u32[]{:S(2)}) %copy-start.1) | copy-done | bytes 65560
  2.4 40.9 %shard_map.50 = (bf16[32,16384]{1,0:T(8,128)(2,1)S(1)}, bf16[32,128]{1,0:T(8,128)(2,1)S(1)}) custom-call(bf16[32,1664]{1,0:T(8,128)(2,1)S(1)} %copy-done, bf16[1664,16384]{1,0:T(8,128)(2,1)} %w_hbm.1, bf16[32,1024]{1,0:T(8,128)(2,1)S(1)} %copy-done.1), custom_call_target="tpu_custom_call" | custom-call | flops 1744830464 | bytes 54525952 | tf_op jit(solution)/shard_map/pallas_call | solution.py:454
  43.2 1.0 %copy.7 = bf16[32,16384]{1,0:T(8,128)(2,1)} copy(bf16[32,16384]{1,0:T(8,128)(2,1)S(1)} %get-tuple-element.4) | data formatting | bytes 2097152
  44.2 0.6 %copy.8 = bf16[32,128]{1,0:T(8,128)(2,1)} copy(bf16[32,128]{1,0:T(8,128)(2,1)S(1)} %get-tuple-element.5) | data formatting | bytes 16384
Async XLA Ops:
  0.6 0.9 %copy-start = (bf16[32,1664]{1,0:T(8,128)(2,1)S(1)}, bf16[32,1664]{1,0:T(8,128)(2,1)}, u32[]{:S(2)}) copy-start(bf16[32,1664]{1,0:T(8,128)(2,1)} %h_hbm.1) | copy-start | bytes 319492
  1.5 0.8 %copy-start.1 = (bf16[32,1024]{1,0:T(8,128)(2,1)S(1)}, bf16[32,1024]{1,0:T(8,128)(2,1)}, u32[]{:S(2)}) copy-start(bf16[32,1024]{1,0:T(8,128)(2,1)} %res_ref.1) | copy-start | bytes 196612

commit v3 on v2

--- a/solution.py
+++ b/solution.py
@@ -12,7 +12,7 @@
 BF16 = jnp.bfloat16
 F32 = jnp.float32
 SLOTS = 16
-DIRECT = 2
+DIRECT = 4
 WIDE_DELAYS = (0, 3, 6, 9, 12, 13)
 NARROW_DELAYS = (0, 3.6, 7.2, 8.2)
 

time: 45 us -> 44.5 us (0.989)
  Pallas kernels: 40.9 us -> 40.3 us
    pallas_call x1, Pallas kernels: 40.9 us -> 40.3 us  [shards(): pl.pallas_call(functools.partial(kernel, n, tuple(scratch)), out_shape=(j...]
where the time goes in v3:
time: 44.5 us; the launch traced here: 44.3 us
  Pallas kernels  40.3 us (91%)
  local copies, waits for them, and re-layouts  3.3 us (7%)
  between operations  0.65 us (1%)
    pallas_call x1, Pallas kernels, shards(): pl.pallas_call(functools.partial(kernel, n, tuple(scratch)), out_shape=(j...  40.3 us
    unnamed x6, local copies, waits for them, and re-layouts  3.3 us

profile of v3, /device:TPU:0, one launch (start us, length us, event | category | flops | bytes accessed | tf_op | source)
XLA Modules:
  0.0 44.3 jit_solution(7956325420247305231)
XLA Ops:
  0.6 0.0 copy-start
  0.6 0.9 %copy-done = bf16[32,1664]{1,0:T(8,128)(2,1)S(1)} copy-done((bf16[32,1664]{1,0:T(8,128)(2,1)S(1)}, bf16[32,1664]{1,0:T(8,128)(2,1)}, u32[]{:S(2)}) %copy-start) | copy-done | bytes 106520
  1.5 0.0 copy-start.1
  1.5 0.8 %copy-done.1 = bf16[32,1024]{1,0:T(8,128)(2,1)S(1)} copy-done((bf16[32,1024]{1,0:T(8,128)(2,1)S(1)}, bf16[32,1024]{1,0:T(8,128)(2,1)}, u32[]{:S(2)}) %copy-start.1) | copy-done | bytes 65560
  2.4 40.3 %shard_map.50 = (bf16[32,16384]{1,0:T(8,128)(2,1)S(1)}, bf16[32,128]{1,0:T(8,128)(2,1)S(1)}) custom-call(bf16[32,1664]{1,0:T(8,128)(2,1)S(1)} %copy-done, bf16[1664,16384]{1,0:T(8,128)(2,1)} %w_hbm.1, bf16[32,1024]{1,0:T(8,128)(2,1)S(1)} %copy-done.1), custom_call_target="tpu_custom_call" | custom-call | flops 1744830464 | bytes 54525952 | tf_op jit(solution)/shard_map/pallas_call | solution.py:454
  42.7 1.0 %copy.7 = bf16[32,16384]{1,0:T(8,128)(2,1)} copy(bf16[32,16384]{1,0:T(8,128)(2,1)S(1)} %get-tuple-element.4) | data formatting | bytes 2097152
  43.7 0.6 %copy.8 = bf16[32,128]{1,0:T(8,128)(2,1)} copy(bf16[32,128]{1,0:T(8,128)(2,1)S(1)} %get-tuple-element.5) | data formatting | bytes 16384
Async XLA Ops:
  0.6 0.9 %copy-start = (bf16[32,1664]{1,0:T(8,128)(2,1)S(1)}, bf16[32,1664]{1,0:T(8,128)(2,1)}, u32[]{:S(2)}) copy-start(bf16[32,1664]{1,0:T(8,128)(2,1)} %h_hbm.1) | copy-start | bytes 319492
  1.5 0.8 %copy-start.1 = (bf16[32,1024]{1,0:T(8,128)(2,1)S(1)}, bf16[32,1024]{1,0:T(8,128)(2,1)}, u32[]{:S(2)}) copy-start(bf16[32,1024]{1,0:T(8,128)(2,1)} %res_ref.1) | copy-start | bytes 196612
